TPU v7x, 512 devices: a whole 4x8x8 slice. The times are simulated.
512 devices in a mesh: dp: 64 (over z_hi, y, core), tensor: 8 (over x, z_lo).
Axes of the slice: x: 4, y: 8, z: 8 (z_hi: 4, z_lo: 2; z = z_hi * 2 + z_lo), core: 2. Of those that a mesh axis runs over, the one named last changes fastest.
Arguments:
- section_input: bfloat16 [2, 8192, 5120], P(None, ('dp', 'tensor')), may hold values from -6 to 6
- w_query: bfloat16 [5120, 8192], P('dp', 'tensor'), may hold values from -0.078125 to 0.078125
- w_kv: bfloat16 [5120, 2, 1024], P(None, None, 'tensor'), may hold values from -0.078125 to 0.078125
- doc_lengths: int32 [64, 2, 4], P('dp'), may hold values from 1 to 64, 128 in all within a row
- d_context: bfloat16 [2, 8192, 8192], P(None, 'dp', 'tensor'), may hold values from -6 to 6
Outputs:
- context: bfloat16 [2, 8192, 8192], P(None, 'dp', 'tensor')
- input_grad: bfloat16 [2, 8192, 5120], P(None, ('dp', 'tensor'))
All inputs are finite; a program needn't handle non-finite values.
Results may differ from a plain program's by a relative error of at most 0.019.
Values may be sent and summed in bfloat16 or wider, within the bound.
A program may use at most 64 MiB of HBM per device.

v0:
```python
import math

import jax
import jax.numpy as jnp
from jax import lax
from jax.sharding import PartitionSpec as P

ROPE_BASE = 1000000.0


def tables(lengths, size, width):
    place = jnp.arange(size, dtype=jnp.int32)
    ends = jnp.cumsum(lengths)
    after = place[:, None] >= ends[None, :]
    docnum = jnp.sum(after.astype(jnp.int32), axis=1)
    begin = jnp.sum(jnp.where(after, lengths[None, :], 0), axis=1)
    offset = (place - begin).astype(jnp.float32)
    half = width // 2
    freq = ROPE_BASE ** (-jnp.arange(half, dtype=jnp.float32) / half)
    angle = offset[:, None] * freq[None, :]
    cosine = jnp.concatenate([jnp.cos(angle), jnp.cos(angle)], axis=1)
    sine = jnp.concatenate([jnp.sin(angle), jnp.sin(angle)], axis=1)
    allowed = (docnum[:, None] == docnum[None, :]) & (place[None, :] <= place[:, None])
    return (cosine, sine, allowed)


def turn(values, cosine, sine):
    half = values.shape[-1] // 2
    rotated = jnp.concatenate([-values[..., half:], values[..., :half]], axis=-1)
    return values * cosine + rotated * sine


def attend(q_raw, k_raw, v_raw, grad_out, lengths):
    size = q_raw.shape[0]
    width = k_raw.shape[1]
    group = q_raw.shape[1] // width
    cosine, sine, allowed = tables(lengths, size, width)
    query = turn(q_raw.reshape(size, group, width), cosine[:, None, :], sine[:, None, :]).astype(
        jnp.bfloat16
    )
    key_rows = turn(k_raw, cosine, sine).astype(jnp.bfloat16)
    value_rows = v_raw.astype(jnp.bfloat16)
    scale = 1.0 / math.sqrt(width)
    scores = jnp.einsum("sgd,td->gst", query, key_rows, preferred_element_type=jnp.float32) * scale
    scores = jnp.where(allowed[None], scores, -1e30)
    top = jnp.max(scores, axis=-1, keepdims=True)
    expo = jnp.exp(scores - top)
    probs = expo / jnp.sum(expo, axis=-1, keepdims=True)
    weights = probs.astype(jnp.bfloat16)
    context = jnp.einsum(
        "gst,td->sgd", weights, value_rows, preferred_element_type=jnp.float32
    ).astype(jnp.bfloat16)
    upstream = grad_out.reshape(size, group, width)
    d_weights = jnp.einsum("sgd,td->gst", upstream, value_rows, preferred_element_type=jnp.float32)
    d_value = jnp.einsum(
        "gst,sgd->td", weights, upstream, preferred_element_type=jnp.float32
    ).astype(jnp.bfloat16)
    d_scores = (
        probs * (d_weights - jnp.sum(probs * d_weights, axis=-1, keepdims=True)) * scale
    ).astype(jnp.bfloat16)
    d_query = turn(
        jnp.einsum("gst,td->sgd", d_scores, key_rows, preferred_element_type=jnp.float32),
        cosine[:, None, :],
        -sine[:, None, :],
    ).astype(jnp.bfloat16)
    d_key = turn(
        jnp.einsum("gst,sgd->td", d_scores, query, preferred_element_type=jnp.float32),
        cosine,
        -sine,
    ).astype(jnp.bfloat16)
    return (
        context.reshape(size, group * width),
        d_query.reshape(size, group * width),
        d_key,
        d_value,
    )


def shards(section_input, w_query, w_kv, doc_lengths, d_context):
    rows = lax.all_gather(section_input, "tensor", axis=1, tiled=True)
    micro, size, width_model = rows.shape
    flat = rows.reshape(micro * size, width_model)
    kv_raw = jnp.einsum("nd,dkc->nkc", flat, w_kv, preferred_element_type=jnp.float32)
    full_query = lax.all_gather(w_query, "dp", axis=0, tiled=True)
    q_raw = jnp.dot(flat, full_query, preferred_element_type=jnp.float32)
    contexts = []
    query_grads = []
    pair_grads = []
    for index in range(micro):
        lower = index * size
        upper = lower + size
        ctx, d_query, d_key, d_value = attend(
            q_raw[lower:upper],
            kv_raw[lower:upper, 0],
            kv_raw[lower:upper, 1],
            d_context[index],
            doc_lengths[0, index],
        )
        contexts.append(ctx)
        query_grads.append(d_query)
        pair_grads.append(jnp.stack([d_key, d_value], axis=1))
    query_flat = jnp.concatenate(query_grads, axis=0)
    pair_flat = jnp.concatenate(pair_grads, axis=0)
    pair_term = jnp.einsum("nkc,dkc->nd", pair_flat, w_kv, preferred_element_type=jnp.float32)
    query_term = jnp.einsum("nc,dc->nd", query_flat, full_query, preferred_element_type=jnp.float32)
    partial_value = (query_term + pair_term).reshape(micro, size, width_model)
    summed = lax.psum_scatter(
        partial_value.astype(jnp.bfloat16), "tensor", scatter_dimension=1, tiled=True
    )
    return (jnp.stack(contexts), summed)


def solution(mesh):
    return jax.shard_map(
        shards,
        mesh=mesh,
        in_specs=(
            P(None, ("dp", "tensor"), None),
            P("dp", "tensor"),
            P(None, None, "tensor"),
            P("dp", None, None),
            P(None, "dp", "tensor"),
        ),
        out_specs=(P(None, "dp", "tensor"), P(None, ("dp", "tensor"), None)),
        check_vma=False,
    )
```

profile of v0, /device:TPU:1, one launch (start us, length us, event | category | flops | bytes accessed | tf_op | source)
XLA Modules:
  0.0 327.4 jit_solution(17638328677145745334)
XLA Ops:
  7.2 0.7 all-gather.3.cloned.1.call-update
  7.9 0.0 all-gather.5.cloned.1.call-start
  8.0 0.7 all-gather.5.cloned.1.call-update
  8.7 0.0 reduce-scatter.2.cloned.1.call-start
  8.7 0.8 slice_bitcast_fusion.4
  9.5 0.2 reduce-window.17
  9.6 0.2 reduce-window.16
  9.8 0.7 convert_reduce_fusion
  10.5 0.9 fusion.103
  11.5 0.2 copy.127
  11.8 1.0 copy.124
  12.8 0.8 copy.135
  13.6 0.2 copy.136
  13.8 5.9 %copy.71 = bf16[5120,2,128]{0,2,1:T(8,128)(2,1)S(1)} copy(bf16[5120,2,128]{2,1,0:T(2,128)(2,1)} %param.7) | data formatting | bytes 5242880 | tf_op args[2]
  19.7 1.5 pad_maximum_fusion.2
  21.2 1.5 pad_maximum_fusion.4
  22.6 0.8 fusion.77
  23.4 1.4 fusion.78
  24.9 1.6 multiply_cosine_fusion.3
  26.4 56.2 %all-gather.3.cloned.1.call-done = bf16[2,128,5120]{2,1,0:T(8,128)(2,1)} async-done(((bf16[2,16,5120]{2,1,0:T(8,128)(2,1)}), bf16[2,128,5120]{2,1,0:T(8,128)(2,1)}) %all-gather.3.cloned.1.call-update) | async-done | bytes 2621456 | tf_op jit(solution)/shard_map/all_gather | solution.py:80
  82.6 2.7 fusion.153
  85.3 0.8 slice_negate_fusion.6
  86.1 1.1 convolution_bitcast_fusion.4
  87.2 1.0 convolution_bitcast_fusion.2
  88.2 110.8 %all-gather.5.cloned.1.call-done = bf16[5120,1024]{1,0:T(8,128)(2,1)} async-done(((bf16[80,1024]{1,0:T(8,128)(2,1)}), bf16[5120,1024]{1,0:T(8,128)(2,1)}) %all-gather.5.cloned.1.call-update) | async-done | bytes 10485776 | tf_op jit(solution)/shard_map/all_gather | solution.py:84
  199.1 6.4 %fusion.154 = f32[256,1024]{1,0:T(8,128)S(1)} fusion(bf16[256,5120]{1,0:T(8,128)(2,1)} %bitcast.214, bf16[5120,1024]{1,0:T(8,128)(2,1)} %all-gather.5.cloned.1.call-done), kind=kOutput, calls=%fused_computation.188 | convolution fusion | flops 2684354560 | bytes 14155776 | tf_op jit(solution)/shard_map/dot_general | solution.py:85
  205.4 1.0 copy-done
  206.4 1.0 fusion.141
  207.5 2.1 copy.133
  209.5 2.0 copy.134
  211.6 1.1 slice_negate_fusion.2
  212.6 1.7 maximum_multiply_fusion.1
  214.3 2.0 copy.128
  216.4 1.1 slice_negate_fusion.3
  217.4 1.7 maximum_multiply_fusion
  219.1 2.0 copy.125
  221.2 2.7 fusion.42
  223.9 2.0 fusion.148
  225.9 0.8 copy-done.19
  226.7 1.8 fusion.25
  228.5 2.8 convolution_bitcast_fusion.8
  231.4 1.4 slice_negate_fusion.5
  232.8 2.8 fusion.143
  235.6 1.9 fusion.24
  237.5 2.1 convolution_bitcast_fusion.6
  239.6 0.6 slice_negate_fusion.4
  240.3 1.9 convolution_bitcast_fusion.1
  242.2 0.7 slice_negate_fusion
  243.0 2.8 convolution_bitcast_fusion.3
  245.8 1.1 slice_negate_fusion.1
  246.9 0.9 fusion.80
  247.8 0.9 fusion.79
  248.7 1.0 fusion.37
  249.8 0.1 fusion.35
  249.9 5.7 %fusion.38 = f32[256,5120]{1,0:T(8,128)S(1)} fusion(bf16[5120,1024]{1,0:T(8,128)(2,1)} %all-gather.5.cloned.1.call-done, bf16[128,1024]{0,1:T(8,128)(2,1)S(1)} %bitcast.200, bf16[128,1024]{0,1:T(8,128)(2,1)S(1)} %bitcast.201), kind=kOutput, calls=%fused_computation.54 | convolution fusion | flops 2685403136 | bytes 16252928 | tf_op jit(solution)/shard_map/nc,dc->nd/dot_general | solution.py:105
  255.6 2.5 fusion.5
  258.2 0.9 copy-done.11
  259.1 0.2 copy-done.20
  259.3 0.2 convolution_convert_fusion.1
  259.5 0.1 copy.86
  259.6 0.2 convolution_convert_fusion
  259.9 0.1 copy.87
  260.0 0.8 pad_maximum_fusion
  260.9 60.0 %reduce-scatter.2.cloned.1.call-done = bf16[2,16,5120]{2,1,0:T(8,128)(2,1)} async-done(((bf16[2,128,5120]{2,1,0:T(8,128)(2,1)}), bf16[2,16,5120]{2,1,0:T(8,128)(2,1)}) %reduce-scatter.2.cloned.1.call-update) | async-done | bytes 327696 | tf_op jit(solution)/shard_map/reduce_scatter | solution.py:107
  (55 shorter events, 0.3 us)
Async XLA Ops:
  7.2 5.6 %copy-start.4 = (bf16[2,128,1024]{2,1,0:T(8,128)(2,1)S(1)}, bf16[2,128,1024]{2,1,0:T(8,128)(2,1)}, u32[]{:S(2)}) copy-start(bf16[2,128,1024]{2,1,0:T(8,128)(2,1)} %param.9) | copy-start | bytes 1572868
  7.2 75.5 %all-gather.3.cloned.1.call-start = ((), (), s32[]{:S(2)}) async-start(), calls=%async_computation.1 | async-start | bytes 2949120 | tf_op jit(solution)/shard_map/all_gather | solution.py:80
  7.9 191.1 %all-gather.5.cloned.1.call-start = ((), (), s32[]{:S(2)}) async-start(), calls=%async_computation.2 | async-start | bytes 10649600 | tf_op jit(solution)/shard_map/all_gather | solution.py:84
  8.7 312.3 %reduce-scatter.2.cloned.1.call-start = ((), (), s32[]{:S(2)}) async-start(), calls=%async_computation.3 | async-start | bytes 2949120 | tf_op jit(solution)/shard_map/reduce_scatter | solution.py:107
  9.8 3.8 %copy-start.16 = (f32[64]{0:T(128)}, f32[64]{0:T(128)S(1)}, u32[]{:S(2)}) copy-start(f32[64]{0:T(128)S(1)} %multiply_power_fusion) | copy-start | bytes 772
  10.5 3.1 copy-start.17
  10.5 3.1 copy-start.18
  11.5 2.2 copy-start.8
  11.5 2.2 copy-start.5
  82.6 3.5 %copy-start.3 = (bf16[1,128,1024]{1,2,0:T(8,128)(2,1)S(1)}, bf16[1,128,1024]{1,2,0:T(8,128)(2,1)}, u32[]{:S(2)}) copy-start(bf16[1,128,1024]{1,2,0:T(8,128)(2,1)} %copy.135) | copy-start | bytes 786436
  85.3 1.9 copy-start.10
  205.4 1.0 copy-start
  225.9 0.8 copy-start.19
  228.5 9.0 %copy-start.1 = (f32[128,1024]{0,1:T(8,128)S(1)}, f32[128,1024]{0,1:T(8,128)}, u32[]{:S(2)}) copy-start(f32[128,1024]{0,1:T(8,128)} %copy.134) | copy-start | bytes 1572868
  235.6 4.6 %copy-start.23 = (f32[8,128]{1,0:T(8,128)S(1)}, f32[8,128]{1,0:T(8,128)}, u32[]{:S(2)}) copy-start(f32[8,128]{1,0:T(8,128)} %get-tuple-element.53) | copy-start | bytes 12292
  237.5 2.7 copy-start.6
  237.5 2.7 copy-start.7
  237.5 2.8 copy-start.12
  237.5 2.8 copy-start.13
  237.5 5.4 %copy-start.22 = (f32[8,128]{1,0:T(8,128)S(1)}, f32[8,128]{1,0:T(8,128)}, u32[]{:S(2)}) copy-start(f32[8,128]{1,0:T(8,128)} %get-tuple-element.55) | copy-start | bytes 12292
  239.6 0.6 copy-start.9
  245.8 4.0 %copy-start.2 = (f32[128,8,128]{0,2,1:T(8,128)S(1)}, f32[128,8,128]{0,2,1:T(8,128)}, u32[]{:S(2)}) copy-start(f32[128,8,128]{0,2,1:T(8,128)} %convolution_bitcast_fusion.3) | copy-start | bytes 1572868
  249.8 5.8 %copy-start.14 = (bf16[128,1,128]{0,2,1:T(8,128)(2,1)S(1)}, bf16[128,1,128]{0,2,1:T(8,128)(2,1)}, u32[]{:S(2)}) copy-start(bf16[128,1,128]{0,2,1:T(8,128)(2,1)} %fusion.25) | copy-start | bytes 98308
  249.9 5.8 %copy-start.15 = (bf16[128,1,128]{0,2,1:T(8,128)(2,1)S(1)}, bf16[128,1,128]{0,2,1:T(8,128)(2,1)}, u32[]{:S(2)}) copy-start(bf16[128,1,128]{0,2,1:T(8,128)(2,1)} %fusion.24) | copy-start | bytes 98308
  258.1 0.9 copy-start.11
  258.1 1.1 copy-start.20
  258.1 1.5 copy-start.21
Sparse Core Ops, SparseCore 0:
  10.1 72.5 all-gather.2
  85.9 113.0 all-gather.4
  258.3 62.5 reduce-scatter.1
where the time goes:
time: 329 us; the launch traced here: 327 us
  waiting for transfers between devices  228 us (69%)
  matrix products  38 us (12%)
  other arithmetic  25.4 us (8%)
  local copies, waits for them, and re-layouts  21.4 us (7%)
  between operations  14.1 us (4%)
    all_gather x1, waiting for transfers between devices, shards(): full_query = lax.all_gather(w_query, 'dp', axis=0, tiled=True)  111 us
    reduce_scatter x1, waiting for transfers between devices, shards(): lax.psum_scatter(partial_value.astype(jnp.bfloat16), 'tensor', scatter_di...  60 us
    all_gather x1, waiting for transfers between devices, shards(): rows = lax.all_gather(section_input, 'tensor', axis=1, tiled=True)  56.2 us
    unnamed x51, local copies, waits for them, and re-layouts  9.83 us
    neg x7, other arithmetic, turn(): -values[..., half:]  6.8 us
  transfers between devices with their start and end apart: 3, of which 3 were waited for; matrix products, arithmetic and copies ran while one was open for 8% of the time, Pallas kernels for 0%

commit v1 on v0

v1 whole, which is shorter than its diff:
```python
import math

import jax
import jax.numpy as jnp
import numpy as np
from jax import lax
from jax.experimental import pallas as pl
from jax.experimental.pallas import tpu as pltpu
from jax.sharding import PartitionSpec as P

ROPE_BASE = 1000000.0
MESH = pl.DeviceIdType.MESH
F32 = jnp.float32
BF16 = jnp.bfloat16

NZ, NY, NX = 4, 8, 4
T = NX * 2
MICRO = 2
LOC = 16
SEQ = T * LOC
D = 5120
HD = 128
GROUP = 8
QC = GROUP * HD
ROWS = 80
PH = 2
PC = QC // PH
HPP = GROUP // PH
NB = 5
DB = D // NB
SCALE = 1.0 / math.sqrt(HD)


def nt(a, b):
    return lax.dot_general(a, b, (((1,), (1,)), ((), ())), preferred_element_type=F32)


def tn(a, b):
    return lax.dot_general(a, b, (((0,), (0,)), ((), ())), preferred_element_type=F32)


def nn(a, b):
    return jnp.dot(a, b, preferred_element_type=F32)


def body(
    x_hbm, w_hbm, kv_hbm, len_ref, dctx_hbm, freq_ref,
    ctx_hbm, grad_hbm,
    xbuf, wbuf, kvi, kvf, wkv, dctx, cos_t, sin_t, mask_t, qraw, kvraw, ctx, dqb, dkvb,
    kbuf, vbuf, dkacc, dvacc, acc, pbuf, accin, accout, fin_m, fin_p, zout, zin, keep, outb,
    loc_sem, wz_s, wz_r, wy_s, wy_r, wc_s, wc_r, x_s, x_r, r_s, r_r,
):
    dp = lax.axis_index("dp")
    t = lax.axis_index("tensor")
    zh, y, c = dp // 16, (dp // 2) % 8, dp % 2
    x, zl = t // 2, t % 2

    def dev(dzh=0, dy=0, dc=0, dx=0, dzl=0):
        a = ((zh + dzh) % NZ) * 16 + ((y + dy) % NY) * 2 + (c + dc) % 2
        return (a, ((x + dx) % NX) * 2 + (zl + dzl) % 2)

    core = dev(dc=1)
    yp, ym = dev(dy=1), dev(dy=-1 + NY)
    zp, zm = dev(dzh=1), dev(dzh=-1 + NZ)
    xp, xm = dev(dx=1), dev(dx=-1 + NX)
    zpair = dev(dzl=1)

    def rows_of(dzh, dy, dc=0):
        a = ((zh + dzh) % NZ) * 16 + ((y + dy) % NY) * 2 + (c + dc) % 2
        return pl.multiple_of(a * ROWS, 16)

    own = rows_of(0, 0)
    load_w = pltpu.make_async_copy(w_hbm, wbuf.at[pl.ds(own, ROWS), :], loc_sem.at[0])
    load_x = pltpu.make_async_copy(x_hbm, xbuf.at[t], loc_sem.at[1])
    load_kv = pltpu.make_async_copy(kv_hbm, kvi, loc_sem.at[2])
    load_d = pltpu.make_async_copy(dctx_hbm, dctx, loc_sem.at[3])
    for cp in (load_w, load_x, load_kv, load_d):
        cp.start()

    bar = pltpu.get_barrier_semaphore()
    for d in (core, yp, ym, zp, zm, xp, xm, zpair):
        pl.semaphore_signal(bar, 1, device_id=d, device_id_type=MESH)
    pl.semaphore_wait(bar, 8)

    def send(src, dst, ss, rs, d):
        pltpu.make_async_remote_copy(
            src_ref=src, dst_ref=dst, send_sem=ss, recv_sem=rs, device_id=d, device_id_type=MESH
        ).start()

    def same(ref, ss, rs, d):
        send(ref, ref, ss, rs, d)

    def got(ref, sem):
        pltpu.make_async_copy(ref, ref, sem).wait()

    def wchunk(dzh, dy, p, part=None):
        col, width = p * PC, PC
        if part is not None:
            width = PC // 2
            col = col + part * width
        return wbuf.at[pl.ds(rows_of(dzh, dy), ROWS), pl.ds(col, width)]

    zoff = (0, NZ - 1, 1, 2)

    def start_z(p):
        ref = wchunk(0, 0, p)
        same(ref, wz_s.at[p], wz_r.at[p, 0], zp)
        same(ref, wz_s.at[p], wz_r.at[p, 1], zm)

    def start_y(p, j):
        ref = wchunk(zoff[j], 0, p)
        same(ref, wy_s.at[p], wy_r.at[p, j, 0, 0], yp)
        same(ref, wy_s.at[p], wy_r.at[p, j, 0, 1], ym)
        same(ref, wc_s.at[p], wc_r.at[p], core)

    def step_z1(p):
        got(wchunk(NZ - 1, 0, p), wz_r.at[p, 0])
        same(wchunk(NZ - 1, 0, p, 0), wz_s.at[p], wz_r.at[p, 2], zp)
        got(wchunk(1, 0, p), wz_r.at[p, 1])
        same(wchunk(1, 0, p, 1), wz_s.at[p], wz_r.at[p, 3], zm)

    def step_z2(p):
        got(wchunk(2, 0, p, 0), wz_r.at[p, 2])
        got(wchunk(2, 0, p, 1), wz_r.at[p, 3])

    def step_y(p, j, h):
        o = zoff[j]
        if h < 4:
            lo, hi = wchunk(o, NY - h, p), wchunk(o, h, p)
            got(lo, wy_r.at[p, j, h - 1, 0])
            if h < 3:
                same(lo, wy_s.at[p], wy_r.at[p, j, h, 0], yp)
            else:
                same(wchunk(o, NY - h, p, 0), wy_s.at[p], wy_r.at[p, j, h, 0], yp)
            same(lo, wc_s.at[p], wc_r.at[p], core)
            got(hi, wy_r.at[p, j, h - 1, 1])
            if h < 3:
                same(hi, wy_s.at[p], wy_r.at[p, j, h, 1], ym)
            else:
                same(wchunk(o, h, p, 1), wy_s.at[p], wy_r.at[p, j, h, 1], ym)
            same(hi, wc_s.at[p], wc_r.at[p], core)
        else:
            got(wchunk(o, 4, p, 0), wy_r.at[p, j, 3, 0])
            got(wchunk(o, 4, p, 1), wy_r.at[p, j, 3, 1])
            same(wchunk(o, 4, p), wc_s.at[p], wc_r.at[p], core)

    def core_done(p):
        ref = wbuf.at[pl.ds(0, D // 2), pl.ds(p * PC, PC)]
        got(ref, wc_r.at[p])

    def xrow(dx, dzl):
        return ((x + dx) % NX) * 2 + (zl + dzl) % 2

    def start_x(b):
        r = xbuf.at[xrow(0, b)]
        same(r, x_s.at[1 + b], x_r.at[1 + 4 * b], xp)
        same(r, x_s.at[1 + b], x_r.at[2 + 4 * b], xm)

    def start_xz():
        same(xbuf.at[t], x_s.at[0], x_r.at[0], zpair)

    def step_xz():
        got(xbuf.at[xrow(0, 1)], x_r.at[0])
        start_x(1)

    def step_x1(b):
        r = xrow(NX - 1, b)
        got(xbuf.at[r], x_r.at[1 + 4 * b])
        same(xbuf.at[r, 0], x_s.at[1 + b], x_r.at[3 + 4 * b], xp)
        r = xrow(1, b)
        got(xbuf.at[r], x_r.at[2 + 4 * b])
        same(xbuf.at[r, 1], x_s.at[1 + b], x_r.at[4 + 4 * b], xm)

    def step_x2(b):
        r = xrow(2, b)
        got(xbuf.at[r, 0], x_r.at[3 + 4 * b])
        got(xbuf.at[r, 1], x_r.at[4 + 4 * b])

    def make_tables():
        lanes = lax.broadcasted_iota(jnp.int32, (SEQ, HD), 1)
        place = lax.broadcasted_iota(jnp.int32, (SEQ, HD), 0)
        sign = jnp.where(lanes < HD // 2, -1.0, 1.0).astype(F32)
        freq = freq_ref[0:1, :]
        for m in range(MICRO):
            end = jnp.int32(0)
            begin = jnp.zeros((SEQ, HD), jnp.int32)
            doc_s = jnp.zeros((SEQ, HD), jnp.int32)
            doc_t = jnp.zeros((SEQ, HD), jnp.int32)
            for k in range(4):
                length = len_ref[0, m, k]
                end = end + length
                after = place >= end
                begin = begin + jnp.where(after, length, 0)
                doc_s = doc_s + after.astype(jnp.int32)
                doc_t = doc_t + (lanes >= end).astype(jnp.int32)
            angle = (place - begin).astype(F32) * freq
            cos_t[m] = jnp.cos(angle)
            sin_t[m] = jnp.sin(angle) * sign
            mask_t[m] = jnp.where((doc_s == doc_t) & (lanes <= place), 1.0, 0.0).astype(F32)

    def split_kv(i):
        n = D // 8

        def one(k, _):
            kvf[...] = kvi[pl.ds(pl.multiple_of(k * 2 * n, 16), 2 * n), :].astype(F32)
            at = pl.ds(pl.multiple_of(k * n, 16), n)
            wkv[at, 0:HD] = kvf[pl.ds(0, n, stride=2), :].astype(BF16)
            wkv[at, HD:2 * HD] = kvf[pl.ds(1, n, stride=2), :].astype(BF16)
            return 0

        lax.fori_loop(2 * i, 2 * i + 2, one, 0)

    def turn(v, m, back=False):
        rolled = pltpu.roll(v, HD // 2, 1) * sin_t[m]
        return v * cos_t[m] - rolled if back else v * cos_t[m] + rolled

    KB = 1024

    def kv_mm():
        total = jnp.zeros((T * MICRO * LOC, 2 * HD), F32)
        for k in range(D // KB):
            rows = xbuf[:, :, :, k * KB:(k + 1) * KB].reshape(T * MICRO * LOC, KB)
            total = total + nn(rows, wkv[k * KB:(k + 1) * KB, :])
        kvraw[...] = total.reshape(T, MICRO, LOC, 2 * HD)
        for m in range(MICRO):
            kr = kvraw[:, m, :, 0:HD].reshape(SEQ, HD)
            kbuf[m] = turn(kr, m).astype(BF16)
            vbuf[m] = kvraw[:, m, :, HD:2 * HD].reshape(SEQ, HD).astype(BF16)

    def q_mm(p, k):
        rows = xbuf[:, :, :, k * KB:(k + 1) * KB].reshape(T * MICRO * LOC, KB)
        part = nn(rows, wbuf[k * KB:(k + 1) * KB, p * PC:(p + 1) * PC])
        part = part.reshape(T, MICRO, LOC, PC)
        if k == 0:
            qraw[...] = part
        else:
            qraw[...] += part

    def attend(p, m):
        key, val = kbuf[m], vbuf[m]
        queries, ups = [], []
        for h in range(HPP):
            qr = qraw[:, m, :, h * HD:(h + 1) * HD].reshape(SEQ, HD)
            queries.append(turn(qr, m).astype(BF16))
            g = p * HPP + h
            ups.append(dctx[m, :, g * HD:(g + 1) * HD])
        query = jnp.concatenate(queries, axis=0)
        up = jnp.concatenate(ups, axis=0)
        mask = jnp.concatenate([mask_t[m]] * HPP, axis=0) > 0.5
        s = jnp.where(mask, nt(query, key) * SCALE, -1e30)
        e = jnp.exp(s - jnp.max(s, axis=1, keepdims=True))
        probs = e / jnp.sum(e, axis=1, keepdims=True)
        w = probs.astype(BF16)
        out = nn(w, val).astype(BF16)
        dw = nt(up, val)
        ds = (probs * (dw - jnp.sum(probs * dw, axis=1, keepdims=True)) * SCALE).astype(BF16)
        dv = tn(w, up)
        dk = tn(ds, query)
        if p == 0:
            dvacc[m] = dv
            dkacc[m] = dk
        else:
            dvacc[m] += dv
            dkacc[m] += dk
        dq = nn(ds, key)
        for h in range(HPP):
            g = p * HPP + h
            at = slice(g * HD, (g + 1) * HD)
            ctx[m, :, at] = out[h * SEQ:(h + 1) * SEQ]
            piece = turn(dq[h * SEQ:(h + 1) * SEQ], m, True).astype(BF16)
            dqb[:, m, :, at] = piece.reshape(T, LOC, HD)
        if p == PH - 1:
            dk = turn(dkacc[m], m, True).astype(BF16)
            dkvb[:, m, :, 0:HD] = dk.reshape(T, LOC, HD)
            dkvb[:, m, :, HD:2 * HD] = dvacc[m].astype(BF16).reshape(T, LOC, HD)

    def back_first(k):
        at = slice(k * DB, (k + 1) * DB)
        lhs = dqb[:, :, :, 0:PC].reshape(T * MICRO * LOC, PC)
        acc[:, at] = nt(lhs, wbuf[at, 0:PC])

    def back_last(k):
        at = slice(k * DB, (k + 1) * DB)
        lhs = dqb[:, :, :, PC:].reshape(T * MICRO * LOC, PC)
        lkv = dkvb[...].reshape(T * MICRO * LOC, 2 * HD)
        total = acc[:, at] + nt(lhs, wbuf[at, PC:]) + nt(lkv, wkv[at, :])
        pbuf[:, at] = total.astype(BF16)

    XR = 2 * MICRO * LOC

    def xrows(dx):
        return pl.ds(pl.multiple_of(((x + dx) % NX) * XR, 16), XR)

    def halves(b):
        half = DB // 2
        return pl.ds(b * DB, half), pl.ds(b * DB + half, half)

    def rs_start(b):
        ca, cb = halves(b)
        send(pbuf.at[xrows(2), ca], accin.at[:, ca], r_s.at[0], r_r.at[b, 0], xp)
        send(pbuf.at[xrows(2), cb], accin.at[:, cb], r_s.at[0], r_r.at[b, 1], xm)
        send(pbuf.at[xrows(1), cb], fin_m.at[:, cb], r_s.at[0], r_r.at[b, 2], xp)
        send(pbuf.at[xrows(NX - 1), ca], fin_p.at[:, ca], r_s.at[0], r_r.at[b, 3], xm)

    def rs_add(b):
        ca, cb = halves(b)
        got(accin.at[:, ca], r_r.at[b, 0])
        accout[:, ca] = (accin[:, ca].astype(F32) + pbuf[xrows(1), ca].astype(F32)).astype(BF16)
        send(accout.at[:, ca], fin_m.at[:, ca], r_s.at[0], r_r.at[b, 4], xp)
        got(accin.at[:, cb], r_r.at[b, 1])
        accout[:, cb] = (accin[:, cb].astype(F32) + pbuf[xrows(NX - 1), cb].astype(F32)).astype(BF16)
        send(accout.at[:, cb], fin_p.at[:, cb], r_s.at[0], r_r.at[b, 5], xm)

    ZR = MICRO * LOC

    def rs_join(b):
        ca, cb = halves(b)
        full = pl.ds(b * DB, DB)
        got(fin_m.at[:, cb], r_r.at[b, 2])
        got(fin_p.at[:, ca], r_r.at[b, 3])
        got(fin_m.at[:, ca], r_r.at[b, 4])
        got(fin_p.at[:, cb], r_r.at[b, 5])
        mine = pl.ds(pl.multiple_of(zl * ZR, 16), ZR)
        theirs = pl.ds(pl.multiple_of((1 - zl) * ZR, 16), ZR)

        def total(rows, which):
            return (
                fin_m[which, full].astype(F32) + fin_p[which, full].astype(F32)
                + pbuf[rows, full].astype(F32)
            )

        base = ((x % NX) * 2) * ZR
        zout[:, full] = total(pl.ds(pl.multiple_of(base + (1 - zl) * ZR, 16), ZR), theirs).astype(BF16)
        send(zout.at[:, full], zin.at[:, full], r_s.at[1], r_r.at[b, 6], zpair)
        keep[:, full] = total(pl.ds(pl.multiple_of(base + zl * ZR, 16), ZR), mine)

    def rs_last(b):
        full = pl.ds(b * DB, DB)
        got(zin.at[:, full], r_r.at[b, 6])
        res = (keep[:, full] + zin[:, full].astype(F32)).astype(BF16)
        outb[:, :, full] = res.reshape(MICRO, LOC, DB)

    load_w.wait()
    start_y(0, 0)
    start_z(0)
    load_x.wait()
    start_x(0)
    start_xz()
    make_tables()
    load_kv.wait()
    step_y(0, 0, 1)
    start_y(1, 0)
    step_z1(0)
    start_y(0, 1)
    start_y(0, 2)
    step_y(0, 0, 2)
    step_x1(0)
    step_z2(0)
    start_y(0, 3)
    start_z(1)
    split_kv(0)
    step_y(0, 1, 1)
    step_y(0, 2, 1)
    step_xz()
    step_y(0, 0, 3)
    step_y(0, 3, 1)
    split_kv(1)
    step_y(0, 1, 2)
    step_y(0, 2, 2)
    step_x2(0)
    step_y(0, 0, 4)
    step_z1(1)
    step_y(0, 3, 2)
    split_kv(2)
    step_y(1, 0, 1)
    step_x1(1)
    step_y(0, 1, 3)
    step_y(0, 2, 3)
    start_y(1, 1)
    start_y(1, 2)
    step_z2(1)
    step_y(0, 3, 3)
    start_y(1, 3)
    split_kv(3)
    step_x2(1)
    step_y(0, 1, 4)
    step_y(0, 2, 4)
    step_y(0, 3, 4)
    core_done(0)
    load_d.wait()

    pieces = [kv_mm]
    pieces += [lambda k=k: q_mm(0, k) for k in range(D // KB)]
    pieces += [lambda m=m: attend(0, m) for m in range(MICRO)]
    pieces += [lambda k=k: back_first(k) for k in range(NB)]
    steps = [(0, 2), (1, 1), (2, 1), (3, 1), (0, 3), (1, 2), (2, 2), (3, 2), (0, 4), (1, 3), (2, 3), (3, 3), (1, 4), (2, 4), (3, 4)]
    while steps or pieces:
        if steps:
            j, h = steps.pop(0)
            step_y(1, j, h)
        if pieces:
            pieces.pop(0)()
    core_done(1)
    for k in range(D // KB):
        q_mm(1, k)
    for m in range(MICRO):
        attend(1, m)
    put_ctx = pltpu.make_async_copy(ctx, ctx_hbm, loc_sem.at[4])
    put_ctx.start()
    for b in range(NB):
        back_last(b)
        rs_start(b)
    for b in range(NB):
        rs_add(b)
        if b > 0:
            rs_join(b - 1)
        if b > 1:
            rs_last(b - 2)
    rs_join(NB - 1)
    rs_last(NB - 2)
    rs_last(NB - 1)
    put_grad = pltpu.make_async_copy(outb, grad_hbm, loc_sem.at[5])
    put_grad.start()

    def sent(n_rows, n_cols, sem):
        got(wbuf.at[pl.ds(0, n_rows), pl.ds(0, n_cols)], sem)

    for p in range(PH):
        sent(3 * ROWS, PC, wz_s.at[p])
        sent(28 * ROWS, PC, wy_s.at[p])
        sent(32 * ROWS, PC, wc_s.at[p])
    got(xbuf.at[0], x_s.at[0])
    for b in range(2):
        got(xbuf.at[pl.ds(0, 3)], x_s.at[1 + b])
    got(pbuf.at[pl.ds(0, 3 * XR), :], r_s.at[0])
    got(zout, r_s.at[1])
    put_ctx.wait()
    put_grad.wait()


def run(x_in, w_in, kv_in, lens, d_in):
    half = HD // 2
    freq = (ROPE_BASE ** (-np.arange(half, dtype=np.float32) / np.float32(half))).astype(np.float32)
    freq = jnp.asarray(np.broadcast_to(np.concatenate([freq, freq])[None], (8, HD)))
    kv2 = kv_in.reshape(2 * D, HD)
    anyspec = pl.BlockSpec(memory_space=pl.ANY)
    dma, vm = pltpu.SemaphoreType.DMA, pltpu.VMEM
    scratch = [
        vm((T, MICRO, LOC, D), BF16),
        vm((D, QC), BF16),
        vm((2 * D, HD), BF16),
        vm((2 * D // 8, HD), F32),
        vm((D, 2 * HD), BF16),
        vm((MICRO, SEQ, QC), BF16),
        vm((MICRO, SEQ, HD), F32),
        vm((MICRO, SEQ, HD), F32),
        vm((MICRO, SEQ, HD), F32),
        vm((T, MICRO, LOC, PC), F32),
        vm((T, MICRO, LOC, 2 * HD), F32),
        vm((MICRO, SEQ, QC), BF16),
        vm((T, MICRO, LOC, QC), BF16),
        vm((T, MICRO, LOC, 2 * HD), BF16),
        vm((MICRO, SEQ, HD), BF16),
        vm((MICRO, SEQ, HD), BF16),
        vm((MICRO, SEQ, HD), F32),
        vm((MICRO, SEQ, HD), F32),
        vm((T * MICRO * LOC, D), F32),
        vm((T * MICRO * LOC, D), BF16),
        vm((2 * MICRO * LOC, D), BF16),
        vm((2 * MICRO * LOC, D), BF16),
        vm((2 * MICRO * LOC, D), BF16),
        vm((2 * MICRO * LOC, D), BF16),
        vm((MICRO * LOC, D), BF16),
        vm((MICRO * LOC, D), BF16),
        vm((MICRO * LOC, D), F32),
        vm((MICRO, LOC, D), BF16),
        dma((6,)),
        dma((PH,)),
        dma((PH, 4)),
        dma((PH,)),
        dma((PH, 4, 4, 2)),
        dma((PH,)),
        dma((PH,)),
        dma((3,)),
        dma((9,)),
        dma((2,)),
        dma((NB, 7)),
    ]
    return pl.pallas_call(
        body,
        name="layer",
        out_shape=(
            jax.ShapeDtypeStruct((MICRO, SEQ, QC), BF16),
            jax.ShapeDtypeStruct((MICRO, LOC, D), BF16),
        ),
        in_specs=[
            anyspec, anyspec, anyspec, pl.BlockSpec(memory_space=pltpu.SMEM), anyspec,
            pl.BlockSpec(memory_space=pltpu.VMEM),
        ],
        out_specs=(anyspec, anyspec),
        scratch_shapes=scratch,
        compiler_params=pltpu.CompilerParams(
            collective_id=0, has_side_effects=True, vmem_limit_bytes=56 << 20
        ),
        cost_estimate=pl.CostEstimate(flops=7_500_000_000, bytes_accessed=5_000_000, transcendentals=1_000_000),
    )(x_in, w_in, kv2, lens, d_in, freq)


def solution(mesh):
    return jax.shard_map(
        run,
        mesh=mesh,
        in_specs=(
            P(None, ("dp", "tensor"), None),
            P("dp", "tensor"),
            P(None, None, "tensor"),
            P("dp", None, None),
            P(None, "dp", "tensor"),
        ),
        out_specs=(P(None, "dp", "tensor"), P(None, ("dp", "tensor"), None)),
        check_vma=False,
    )
```

time: 329 us -> 113 us (0.34)
  waiting for transfers between devices: 228 us -> 0 us
  Pallas kernels: 0 us -> 107 us
  matrix products: 38 us -> 0 us
  other arithmetic: 25.4 us -> 0 us
  local copies, waits for them, and re-layouts: 21.4 us -> 4.84 us
  between operations: 14.1 us -> 0.64 us
    all_gather x2 -> x0, waiting for transfers between devices: 167 us -> none  [the longest x1 111 us: shards(): full_query = lax.all_gather(w_query, 'dp', axis=0, tiled=True)]
    pallas_call x0 -> x1, Pallas kernels: none -> 107 us  [run(): pl.pallas_call(body, name='layer', out_shape=(jax.ShapeDtypeStruct((MICRO...]
    reduce_scatter x1 -> x0, waiting for transfers between devices: 60 us -> none  [shards(): lax.psum_scatter(partial_value.astype(jnp.bfloat16), 'tensor', scatter_di...]
    dot_general x13 -> x0, matrix products: 30.5 us -> none  [the longest x1 6.37 us: shards(): q_raw = jnp.dot(flat, full_query, preferred_element_type=jnp.float32)]
    neg x7 -> x0, other arithmetic: 6.8 us -> none  [turn(): -values[..., half:]]
    unnamed x51 -> x2, local copies, waits for them, and re-layouts: 9.83 us -> 3.59 us
    mul x6 -> x0, local copies, waits for them, and re-layouts: 5.33 us -> none  [turn(): return values * cosine + rotated * sine]
    sub x2 -> x0, matrix products: 4.84 us -> none  [attend(): expo = jnp.exp(scores - top)]
  transfers between devices with their start and end apart: 3 -> 0, of which waited for: 3 -> 0; matrix products, arithmetic and copies ran while one was open for 8% -> 0% of each run, Pallas kernels for 0% -> 0%
where the time goes in v1:
time: 113 us; the launch traced here: 112 us
  Pallas kernels  107 us (95%)
  local copies, waits for them, and re-layouts  4.84 us (4%)
    pallas_call x1, Pallas kernels, run(): pl.pallas_call(body, name='layer', out_shape=(jax.ShapeDtypeStruct((MICRO...  107 us
    unnamed x2, local copies, waits for them, and re-layouts  3.59 us

profile of v1, /device:TPU:1, one launch (start us, length us, event | category | flops | bytes accessed | tf_op | source)
XLA Modules:
  0.0 112.4 jit_solution(11983106121866108240)
XLA Ops:
  0.6 1.3 %jit_solution_.3.freq_ref = f32[8,128]{1,0:T(8,128)} broadcast(f32[128]{0:T(128)} %constant.2.clone), dimensions={1} | broadcast | bytes 4608 | tf_op jit(solution)
  1.9 107.0 %layer.1 = (bf16[2,128,1024]{2,1,0:T(8,128)(2,1)}, bf16[2,16,5120]{2,1,0:T(8,128)(2,1)}) custom-call(bf16[2,16,5120]{2,1,0:T(8,128)(2,1)} %x_hbm.1, bf16[80,1024]{1,0:T(8,128)(2,1)} %w_hbm.1, bf16[10240,128]{1,0:T(8,128)(2,1)} %bitcast.1, s32[1,2,4]{2,1,0:T(2,128)} %len_ref.1, bf16[2,128,1024]{2,1,0:T(8,128)(2,1)} %dctx_hbm.1, f32[8,128]{1,0:T(8,128)} %jit_solution_.3.freq_ref), custom_call_target="tpu_custom_call" | custom-call | flops 7500000256 | bytes 5000000 | tf_op jit(solution)/shard_map/layer/pallas_call | solution.py:489
  108.9 1.9 %copy.10 = bf16[2,128,1024]{2,1,0:T(8,128)(2,1)} copy(bf16[2,128,1024]{2,1,0:T(8,128)(2,1)} %get-tuple-element.4) | data formatting | bytes 1048576
  110.7 1.7 %copy.11 = bf16[2,16,5120]{2,1,0:T(8,128)(2,1)} copy(bf16[2,16,5120]{2,1,0:T(8,128)(2,1)} %get-tuple-element.5) | data formatting | bytes 655360

commit v2 on v1

v2 whole, which is shorter than its diff:
```python
import math

import jax
import jax.numpy as jnp
from jax import lax
from jax.experimental import pallas as pl
from jax.experimental.pallas import tpu as pltpu
from jax.sharding import PartitionSpec as P

ROPE_BASE = 1000000.0
MESH = pl.DeviceIdType.MESH
F32 = jnp.float32
BF16 = jnp.bfloat16

NZ, NY, NX = 4, 8, 4
T = NX * 2
MICRO = 2
LOC = 16
SEQ = T * LOC
D = 5120
HD = 128
GROUP = 8
QC = GROUP * HD
ROWS = 80
PW = (384, 256, 128)
QW = (128, 128, 0)
PC = tuple(u + v for u, v in zip(PW, QW))
PH = len(PW)
HP = tuple(v // HD for v in PC)
COL = tuple(sum(PC[:i]) for i in range(PH + 1))
NB = 8
DB = D // NB
KB = D // NZ
SCALE = 1.0 / math.sqrt(HD)
ZFIRST = (1, 2, 3)
ORDER = (
    ("qo", 0), ("xo",), ("zo", 0), ("xp",), ("yo", 0), ("tab",), ("qy", 0, 1), ("qo", 1), ("yo", 1),
    ("kvs", 0), ("ys", 0, 0, 1), ("kvs", 1), ("qy", 0, 2), ("yo", 2), ("z1", 0), ("yz", 0, 1), ("yz", 0, 2),
    ("qy", 1, 1), ("ys", 1, 0, 1), ("kvs", 2), ("kvs", 3), ("qy", 0, 3), ("ys", 0, 0, 2), ("zo", 1),
    ("x1", 0), ("ys", 2, 0, 1), ("xz",), ("z2", 0), ("yz", 0, 3), ("ys", 0, 1, 1), ("ys", 0, 2, 1),
    ("qy", 1, 2), ("ys", 1, 0, 2), ("qy", 0, 4), ("qz", 0, 0), ("z1", 1), ("ys", 0, 0, 3), ("x2", 0),
    ("ys", 2, 0, 2), ("ys", 0, 3, 1), ("ys", 0, 1, 2), ("ys", 0, 2, 2), ("qy", 1, 3), ("ys", 1, 0, 3),
    ("ys", 0, 0, 4), ("zo", 2), ("ys", 2, 0, 3), ("x1", 1), ("ys", 0, 3, 2), ("qz", 0, 1), ("ys", 0, 1, 3),
    ("z2", 1), ("z1", 2), ("yz", 1, 1), ("ys", 0, 2, 3), ("qy", 1, 4), ("qz", 1, 0), ("ys", 1, 0, 4),
    ("ys", 2, 0, 4), ("yz", 1, 2), ("x2", 1), ("kvm",), ("ys", 0, 1, 4), ("ys", 0, 3, 3), ("yz", 1, 3),
    ("ys", 1, 1, 1), ("qz", 0, 2), ("ys", 0, 2, 4), ("z2", 2), ("yz", 2, 1), ("yz", 2, 2), ("ys", 1, 2, 1),
    ("ys", 0, 3, 4), ("yz", 2, 3), ("ys", 1, 3, 1), ("cd", 0), ("qm", 0, 0), ("ys", 1, 1, 2), ("qm", 0, 1),
    ("ys", 2, 1, 1), ("ys", 2, 2, 1), ("qm", 0, 2), ("qm", 0, 3), ("ys", 1, 2, 2), ("at", 0, 0),
    ("ys", 2, 3, 1), ("ys", 1, 3, 2), ("at", 0, 1), ("qz", 1, 1), ("ys", 1, 1, 3), ("ys", 2, 1, 2),
    ("ys", 2, 2, 2), ("bf", 0, 0), ("bf", 0, 1), ("ys", 1, 2, 3), ("bf", 0, 2), ("ys", 2, 3, 2), ("bf", 0, 3),
    ("bf", 0, 4), ("ys", 1, 3, 3), ("bf", 0, 5), ("ys", 1, 1, 4), ("bf", 0, 6), ("ys", 2, 1, 3), ("bf", 0, 7),
    ("ys", 2, 2, 3), ("ys", 1, 2, 4), ("ys", 2, 3, 3), ("ys", 1, 3, 4), ("ys", 2, 1, 4), ("qz", 1, 2),
    ("ys", 2, 2, 4), ("ys", 2, 3, 4), ("cd", 1), ("qm", 1, 0), ("qm", 1, 1), ("qm", 1, 2), ("cd", 2),
    ("qm", 1, 3), ("at", 1, 0), ("at", 1, 1), ("bf", 1, 0), ("bf", 1, 1), ("bf", 1, 2), ("bf", 1, 3),
    ("bf", 1, 4), ("bf", 1, 5), ("bf", 1, 6), ("bf", 1, 7), ("qm", 2, 0), ("qm", 2, 1), ("qm", 2, 2),
    ("qm", 2, 3), ("at", 2, 0), ("at", 2, 1), ("bl", 0), ("bl", 1), ("bl", 2), ("bl", 3), ("bl", 4),
    ("bl", 5), ("bl", 6), ("bl", 7), ("rb", 0), ("rb", 4), ("zj", 1), ("rb", 5), ("rb", 6), ("zj", 2),
    ("rb", 7), ("rj", 0), ("rj", 4), ("zj", 3), ("rb", 1), ("rj", 5), ("rl", 0), ("rj", 6), ("rl", 4),
    ("rb", 2), ("rj", 7), ("rl", 5), ("rb", 3), ("rl", 6), ("rj", 1), ("rj", 2), ("rl", 7), ("rj", 3),
)


def nt(a, b):
    return lax.dot_general(a, b, (((1,), (1,)), ((), ())), preferred_element_type=F32)


def tn(a, b):
    return lax.dot_general(a, b, (((0,), (0,)), ((), ())), preferred_element_type=F32)


def nn(a, b):
    return jnp.dot(a, b, preferred_element_type=F32)


def body(
    x_hbm, w_hbm, kv_hbm, len_ref, dctx_hbm,
    ctx_hbm, grad_hbm,
    xbuf, wb0, wb1, wb2, kvi, kvf, wkv, dctx, cos_t, sin_t, mask_t, qraw, kvraw, ctx, dqb, dkvb,
    kbuf, vbuf, dkacc, dvacc, acc, pbuf, accin, accout, fin_m, fin_p, zout, zin, zinb, keep, outb,
    loc_sem, wz_s, wz_r, wy_s, wy_r, qy_s, qy_r, qz_s, qz_r, wc_s, wc_r, x_s, x_r, r_s, r_r,
):
    wbuf = (wb0, wb1, wb2)
    dp = lax.axis_index("dp")
    t = lax.axis_index("tensor")
    zh, y, c = dp // 16, (dp // 2) % 8, dp % 2
    x, zl = t // 2, t % 2

    def dev(dzh=0, dy=0, dc=0, dx=0, dzl=0):
        a = ((zh + dzh) % NZ) * 16 + ((y + dy) % NY) * 2 + (c + dc) % 2
        return (a, ((x + dx) % NX) * 2 + (zl + dzl) % 2)

    core = dev(dc=1)
    yp, ym = dev(dy=1), dev(dy=-1 + NY)
    zp, zm = dev(dzh=1), dev(dzh=-1 + NZ)
    xr, xm = dev(dx=1), dev(dx=-1 + NX)
    zpair = dev(dzl=1)

    load_w = [
        pltpu.make_async_copy(
            w_hbm.at[:, pl.ds(COL[p], PC[p])], wbuf[p].at[zh, y, c], loc_sem.at[6 + p]
        )
        for p in range(PH)
    ]
    load_x = pltpu.make_async_copy(x_hbm, xbuf.at[t], loc_sem.at[1])
    load_kv = pltpu.make_async_copy(kv_hbm, kvi, loc_sem.at[2])
    load_d = pltpu.make_async_copy(dctx_hbm, dctx, loc_sem.at[3])
    for cp in (*load_w, load_x, load_kv, load_d):
        cp.start()

    bar = pltpu.get_barrier_semaphore()
    for d in (core, yp, ym, zp, zm, xr, xm, zpair):
        pl.semaphore_signal(bar, 1, device_id=d, device_id_type=MESH)
    pl.semaphore_wait(bar, 8)

    def send(src, dst, ss, rs, d):
        pltpu.make_async_remote_copy(
            src_ref=src, dst_ref=dst, send_sem=ss, recv_sem=rs, device_id=d, device_id_type=MESH
        ).start()

    def same(ref, ss, rs, d):
        send(ref, ref, ss, rs, d)

    def got(ref, sem):
        pltpu.make_async_copy(ref, ref, sem).wait()

    def zi(dzh):
        return (zh + dzh + NZ) % NZ

    def yi(dy):
        return (y + dy + NY) % NY

    def wchunk(p, dzh, dy, rows=(0, ROWS)):
        return wbuf[p].at[zi(dzh), yi(dy), c, pl.ds(rows[0], rows[1]), pl.ds(0, PW[p])]

    def qchunk(p, dy, rows=(0, ROWS)):
        return wbuf[p].at[zh, yi(dy), c, pl.ds(rows[0], rows[1]), pl.ds(PW[p], QW[p])]

    def qblock(p, dzh, half=None):
        ys = pl.ds(0, NY) if half is None else pl.ds(half * (NY // 2), NY // 2)
        return wbuf[p].at[zi(dzh), ys, c, :, pl.ds(PW[p], QW[p])]

    def cut(n):
        first = 48 if n % 2 == 0 else 32
        return (0, first), (first, ROWS - first)

    zoff = (0, -1, 1, 2)

    def yo(p):
        yz(p, 0)

    def yz(p, j):
        ref = wchunk(p, zoff[j], 0)
        same(ref, wy_s.at[p], wy_r.at[p, j, 0, 0], yp)
        same(ref, wy_s.at[p], wy_r.at[p, j, 0, 1], ym)
        same(ref, wc_s.at[p], wc_r.at[p], core)

    def zo(p):
        ref = wchunk(p, 0, 0)
        same(ref, wz_s.at[p], wz_r.at[p, 0], zp)
        same(ref, wz_s.at[p], wz_r.at[p, 1], zm)

    def z1(p):
        one, two = cut(p)
        got(wchunk(p, -1, 0), wz_r.at[p, 0])
        same(wchunk(p, -1, 0, one), wz_s.at[p], wz_r.at[p, 2], zp)
        got(wchunk(p, 1, 0), wz_r.at[p, 1])
        same(wchunk(p, 1, 0, two), wz_s.at[p], wz_r.at[p, 3], zm)

    def z2(p):
        one, two = cut(p)
        got(wchunk(p, 2, 0, one), wz_r.at[p, 2])
        got(wchunk(p, 2, 0, two), wz_r.at[p, 3])

    def ys(p, j, h):
        o = zoff[j]
        one, two = cut(p + j)
        if h < 4:
            lo, hi = wchunk(p, o, -h), wchunk(p, o, h)
            far = h == 3
            got(lo, wy_r.at[p, j, h - 1, 0])
            same(wchunk(p, o, -h, one) if far else lo, wy_s.at[p], wy_r.at[p, j, h, 0], yp)
            same(lo, wc_s.at[p], wc_r.at[p], core)
            got(hi, wy_r.at[p, j, h - 1, 1])
            same(wchunk(p, o, h, two) if far else hi, wy_s.at[p], wy_r.at[p, j, h, 1], ym)
            same(hi, wc_s.at[p], wc_r.at[p], core)
        else:
            got(wchunk(p, o, 4, one), wy_r.at[p, j, 3, 0])
            got(wchunk(p, o, 4, two), wy_r.at[p, j, 3, 1])
            same(wchunk(p, o, 4), wc_s.at[p], wc_r.at[p], core)

    def qo(p):
        same(qchunk(p, 0), qy_s.at[p], qy_r.at[p, 0, 0], yp)
        same(qchunk(p, 0), qy_s.at[p], qy_r.at[p, 0, 1], ym)

    def qy(p, h):
        one, two = cut(p)
        if h < 4:
            far = h == 3
            got(qchunk(p, -h), qy_r.at[p, h - 1, 0])
            same(qchunk(p, -h, one) if far else qchunk(p, -h), qy_s.at[p], qy_r.at[p, h, 0], yp)
            got(qchunk(p, h), qy_r.at[p, h - 1, 1])
            same(qchunk(p, h, two) if far else qchunk(p, h), qy_s.at[p], qy_r.at[p, h, 1], ym)
        else:
            got(qchunk(p, 4, one), qy_r.at[p, 3, 0])
            got(qchunk(p, 4, two), qy_r.at[p, 3, 1])

    def qz(p, step):
        if step == 0:
            same(qblock(p, 0), qz_s.at[p], qz_r.at[p, 0], zp)
            same(qblock(p, 0), qz_s.at[p], qz_r.at[p, 1], zm)
            same(qblock(p, 0), wc_s.at[p], wc_r.at[p], core)
        elif step == 1:
            got(qblock(p, -1), qz_r.at[p, 0])
            same(qblock(p, -1, 0), qz_s.at[p], qz_r.at[p, 2], zp)
            same(qblock(p, -1), wc_s.at[p], wc_r.at[p], core)
            got(qblock(p, 1), qz_r.at[p, 1])
            same(qblock(p, 1, 1), qz_s.at[p], qz_r.at[p, 3], zm)
            same(qblock(p, 1), wc_s.at[p], wc_r.at[p], core)
        else:
            got(qblock(p, 2, 0), qz_r.at[p, 2])
            got(qblock(p, 2, 1), qz_r.at[p, 3])
            same(qblock(p, 2), wc_s.at[p], wc_r.at[p], core)

    def cd(p):
        got(wbuf[p].at[:, :, 0], wc_r.at[p])

    def xrow(dx, dzl):
        return ((x + dx) % NX) * 2 + (zl + dzl) % 2

    def start_x(b):
        r = xbuf.at[xrow(0, b)]
        same(r, x_s.at[1 + b], x_r.at[1 + 4 * b], xr)
        same(r, x_s.at[1 + b], x_r.at[2 + 4 * b], xm)

    def xp():
        same(xbuf.at[t], x_s.at[0], x_r.at[0], zpair)

    def xz():
        got(xbuf.at[xrow(0, 1)], x_r.at[0])
        start_x(1)

    def x1(b):
        r = xrow(NX - 1, b)
        got(xbuf.at[r], x_r.at[1 + 4 * b])
        same(xbuf.at[r, 0], x_s.at[1 + b], x_r.at[3 + 4 * b], xr)
        r = xrow(1, b)
        got(xbuf.at[r], x_r.at[2 + 4 * b])
        same(xbuf.at[r, 1], x_s.at[1 + b], x_r.at[4 + 4 * b], xm)

    def x2(b):
        r = xrow(2, b)
        got(xbuf.at[r, 0], x_r.at[3 + 4 * b])
        got(xbuf.at[r, 1], x_r.at[4 + 4 * b])

    def tab():
        lanes = lax.broadcasted_iota(jnp.int32, (SEQ, HD), 1)
        place = lax.broadcasted_iota(jnp.int32, (SEQ, HD), 0)
        sign = jnp.where(lanes < HD // 2, -1.0, 1.0).astype(F32)
        index = jnp.where(lanes < HD // 2, lanes, lanes - HD // 2).astype(F32)
        freq = jnp.exp(index * (-math.log(ROPE_BASE) / (HD // 2)))
        for m in range(MICRO):
            end = jnp.int32(0)
            begin = jnp.zeros((SEQ, HD), jnp.int32)
            doc_s = jnp.zeros((SEQ, HD), jnp.int32)
            doc_t = jnp.zeros((SEQ, HD), jnp.int32)
            for k in range(4):
                length = len_ref[0, m, k]
                end = end + length
                after = place >= end
                begin = begin + jnp.where(after, length, 0)
                doc_s = doc_s + after.astype(jnp.int32)
                doc_t = doc_t + (lanes >= end).astype(jnp.int32)
            angle = (place - begin).astype(F32) * freq
            cos_t[m] = jnp.cos(angle)
            sin_t[m] = jnp.sin(angle) * sign
            mask_t[m] = jnp.where((doc_s == doc_t) & (lanes <= place), 1.0, 0.0).astype(F32)

    def kvs(i):
        n = D // 8

        def one(k, _):
            kvf[...] = kvi[pl.ds(pl.multiple_of(k * 2 * n, 16), 2 * n), :].astype(F32)
            at = pl.ds(pl.multiple_of(k * n, 16), n)
            wkv[at, 0:HD] = kvf[pl.ds(0, n, stride=2), :].astype(BF16)
            wkv[at, HD:2 * HD] = kvf[pl.ds(1, n, stride=2), :].astype(BF16)
            return 0

        lax.fori_loop(2 * i, 2 * i + 2, one, 0)

    def turn(v, m, back=False):
        rolled = pltpu.roll(v, HD // 2, 1) * sin_t[m]
        return v * cos_t[m] - rolled if back else v * cos_t[m] + rolled

    def kvm():
        total = jnp.zeros((T * MICRO * LOC, 2 * HD), F32)
        for k in range(D // KB):
            rows = xbuf[:, :, :, k * KB:(k + 1) * KB].reshape(T * MICRO * LOC, KB)
            total = total + nn(rows, wkv[k * KB:(k + 1) * KB, :])
        kvraw[...] = total.reshape(T, MICRO, LOC, 2 * HD)
        for m in range(MICRO):
            kr = kvraw[:, m, :, 0:HD].reshape(SEQ, HD)
            kbuf[m] = turn(kr, m).astype(BF16)
            vbuf[m] = kvraw[:, m, :, HD:2 * HD].reshape(SEQ, HD).astype(BF16)

    def qm(p, k):
        n = PC[p]
        rows = xbuf[:, :, :, k * KB:(k + 1) * KB].reshape(T * MICRO * LOC, KB)
        part = nn(rows, wbuf[p][k].reshape(KB, n)).reshape(T, MICRO, LOC, n)
        if k == 0:
            qraw[:, :, :, 0:n] = part
        else:
            qraw[:, :, :, 0:n] += part

    def at(p, m):
        key, val = kbuf[m], vbuf[m]
        queries, ups = [], []
        for h in range(HP[p]):
            qr = qraw[:, m, :, h * HD:(h + 1) * HD].reshape(SEQ, HD)
            queries.append(turn(qr, m).astype(BF16))
            g = COL[p] // HD + h
            ups.append(dctx[m, :, g * HD:(g + 1) * HD])
        query = jnp.concatenate(queries, axis=0)
        up = jnp.concatenate(ups, axis=0)
        mask = jnp.concatenate([mask_t[m]] * HP[p], axis=0) > 0.5
        s = jnp.where(mask, nt(query, key) * SCALE, -1e30)
        e = jnp.exp(s - jnp.max(s, axis=1, keepdims=True))
        probs = e / jnp.sum(e, axis=1, keepdims=True)
        w = probs.astype(BF16)
        out = nn(w, val).astype(BF16)
        dw = nt(up, val)
        ds = (probs * (dw - jnp.sum(probs * dw, axis=1, keepdims=True)) * SCALE).astype(BF16)
        dv = tn(w, up)
        dk = tn(ds, query)
        if p == 0:
            dvacc[m] = dv
            dkacc[m] = dk
        else:
            dvacc[m] += dv
            dkacc[m] += dk
        dq = nn(ds, key)
        for h in range(HP[p]):
            g = COL[p] // HD + h
            cols = slice(g * HD, (g + 1) * HD)
            ctx[m, :, cols] = out[h * SEQ:(h + 1) * SEQ]
            piece = turn(dq[h * SEQ:(h + 1) * SEQ], m, True).astype(BF16)
            dqb[:, m, :, cols] = piece.reshape(T, LOC, HD)
        if p == PH - 1:
            dk = turn(dkacc[m], m, True).astype(BF16)
            dkvb[:, m, :, 0:HD] = dk.reshape(T, LOC, HD)
            dkvb[:, m, :, HD:2 * HD] = dvacc[m].astype(BF16).reshape(T, LOC, HD)

    def back(p, k):
        lhs = dqb[:, :, :, COL[p]:COL[p + 1]].reshape(T * MICRO * LOC, PC[p])
        half = NY // 2
        lo = (k % 2) * half
        return nt(lhs, wbuf[p][k // 2, lo:lo + half].reshape(DB, PC[p]))

    def bf(p, k):
        cols = slice(k * DB, (k + 1) * DB)
        if p == 0:
            acc[:, cols] = back(p, k)
        else:
            acc[:, cols] += back(p, k)

    ZR = MICRO * LOC

    def xi(dx):
        return (x + dx + NX) % NX

    def at_cols(b):
        return pl.ds(b * DB, DB)

    def part(b, dx, half):
        if b in ZFIRST:
            return pbuf.at[xi(dx), zl, pl.ds(half * LOC, LOC), at_cols(b)]
        return pbuf.at[xi(dx), half, :, at_cols(b)]

    def slot(buf, b, half):
        if b in ZFIRST:
            return buf.at[0, pl.ds(half * LOC, LOC), at_cols(b)]
        return buf.at[half, :, at_cols(b)]

    def ring(b):
        send(part(b, 2, 0), slot(accin, b, 0), r_s.at[b, 0], r_r.at[b, 0], xr)
        send(part(b, 2, 1), slot(accin, b, 1), r_s.at[b, 0], r_r.at[b, 1], xm)
        send(part(b, 1, 1), slot(fin_m, b, 1), r_s.at[b, 0], r_r.at[b, 2], xr)
        send(part(b, -1, 0), slot(fin_p, b, 0), r_s.at[b, 0], r_r.at[b, 3], xm)

    def bl(b):
        cols = slice(b * DB, (b + 1) * DB)
        lkv = dkvb[...].reshape(T * MICRO * LOC, 2 * HD)
        total = acc[:, cols] + back(PH - 1, b) + nt(lkv, wkv[cols, :])
        pbuf[:, :, :, cols] = total.astype(BF16).reshape(NX, 2, ZR, DB)
        if b in ZFIRST:
            send(
                pbuf.at[:, 1 - zl, :, at_cols(b)], zinb.at[:, :, at_cols(b)],
                r_s.at[b, 1], r_r.at[b, 6], zpair,
            )
        else:
            ring(b)

    def zj(b):
        cols = slice(b * DB, (b + 1) * DB)
        got(zinb.at[:, :, at_cols(b)], r_r.at[b, 6])
        mine = pbuf[:, zl, :, cols].astype(F32) + zinb[:, :, cols].astype(F32)
        pbuf[:, zl, :, cols] = mine.astype(BF16)
        ring(b)

    def rb(b):
        for half, dx, to, fin, k in ((0, 1, xr, fin_m, 0), (1, -1, xm, fin_p, 1)):
            got(slot(accin, b, half), r_r.at[b, k])
            both = slot(accin, b, half)[...].astype(F32) + part(b, dx, half)[...].astype(F32)
            slot(accout, b, half)[...] = both.astype(BF16)
            send(slot(accout, b, half), slot(fin, b, half), r_s.at[b, 0], r_r.at[b, 4 + k], to)

    def store(b, res):
        outb[:, :, b * DB:(b + 1) * DB] = res.astype(BF16).reshape(MICRO, LOC, DB)
        at = (slice(None), slice(None), at_cols(b))
        pltpu.make_async_copy(outb.at[at], grad_hbm.at[at], loc_sem.at[5]).start()

    def rj(b):
        cols = slice(b * DB, (b + 1) * DB)
        got(slot(fin_m, b, 1), r_r.at[b, 2])
        got(slot(fin_p, b, 0), r_r.at[b, 3])
        got(slot(fin_m, b, 0), r_r.at[b, 4])
        got(slot(fin_p, b, 1), r_r.at[b, 5])

        def total(w, own):
            return (
                fin_m[w, :, cols].astype(F32) + fin_p[w, :, cols].astype(F32)
                + pbuf[x, own, :, cols].astype(F32)
            )

        if b in ZFIRST:
            store(b, total(0, zl))
        else:
            zout[:, cols] = total(1 - zl, 1 - zl).astype(BF16)
            send(zout.at[:, at_cols(b)], zin.at[:, at_cols(b)], r_s.at[b, 1], r_r.at[b, 6], zpair)
            keep[:, cols] = total(zl, zl)

    def rl(b):
        cols = slice(b * DB, (b + 1) * DB)
        got(zin.at[:, at_cols(b)], r_r.at[b, 6])
        store(b, keep[:, cols] + zin[:, cols].astype(F32))

    for cp in load_w:
        cp.wait()
    load_x.wait()
    run_of = dict(
        yo=yo, yz=yz, zo=zo, z1=z1, z2=z2, ys=ys, qo=qo, qy=qy, qz=qz, cd=cd,
        xo=lambda: start_x(0), xp=xp, xz=xz, x1=x1, x2=x2,
        tab=tab, kvs=kvs, kvm=kvm, qm=qm, at=at, bf=bf, bl=bl, zj=zj, rb=rb, rj=rj, rl=rl,
    )
    put_ctx = pltpu.make_async_copy(ctx, ctx_hbm, loc_sem.at[4])
    for name, *args in ORDER:
        if (name, *args) == ("kvs", 0):
            load_kv.wait()
        if (name, *args) == ("at", 0, 0):
            load_d.wait()
        run_of[name](*args)
        if (name, *args) == ("at", PH - 1, MICRO - 1):
            put_ctx.start()

    for p in range(PH):
        got(wbuf[p].at[pl.ds(0, 3), 0, 0, :, pl.ds(0, PW[p])], wz_s.at[p])
        got(wbuf[p].at[:, pl.ds(0, 7), 0, :, pl.ds(0, PW[p])], wy_s.at[p])
        got(wbuf[p].at[:, :, 0], wc_s.at[p])
        if QW[p]:
            got(wbuf[p].at[0, pl.ds(0, 7), 0, :, pl.ds(PW[p], QW[p])], qy_s.at[p])
            got(wbuf[p].at[pl.ds(0, 3), :, 0, :, pl.ds(PW[p], QW[p])], qz_s.at[p])
    got(xbuf.at[0], x_s.at[0])
    for b in range(2):
        got(xbuf.at[pl.ds(0, 3)], x_s.at[1 + b])
    for b in range(NB):
        if b in ZFIRST:
            got(pbuf.at[pl.ds(0, 3), 0, :, at_cols(b)], r_s.at[b, 0])
            got(pbuf.at[:, 0, :, at_cols(b)], r_s.at[b, 1])
        else:
            got(pbuf.at[pl.ds(0, 3), :, :, at_cols(b)], r_s.at[b, 0])
            got(pbuf.at[0, 0, :, at_cols(b)], r_s.at[b, 1])
    put_ctx.wait()
    got(outb, loc_sem.at[5])


def run(x_in, w_in, kv_in, lens, d_in):
    kv2 = kv_in.reshape(2 * D, HD)
    anyspec = pl.BlockSpec(memory_space=pl.ANY)
    dma, vm = pltpu.SemaphoreType.DMA, pltpu.VMEM
    scratch = [
        vm((T, MICRO, LOC, D), BF16),
        *[vm((NZ, NY, 2, ROWS, PC[p]), BF16) for p in range(PH)],
        vm((2 * D, HD), BF16),
        vm((2 * D // 8, HD), F32),
        vm((D, 2 * HD), BF16),
        vm((MICRO, SEQ, QC), BF16),
        vm((MICRO, SEQ, HD), F32),
        vm((MICRO, SEQ, HD), F32),
        vm((MICRO, SEQ, HD), F32),
        vm((T, MICRO, LOC, PC[0]), F32),
        vm((T, MICRO, LOC, 2 * HD), F32),
        vm((MICRO, SEQ, QC), BF16),
        vm((T, MICRO, LOC, QC), BF16),
        vm((T, MICRO, LOC, 2 * HD), BF16),
        vm((MICRO, SEQ, HD), BF16),
        vm((MICRO, SEQ, HD), BF16),
        vm((MICRO, SEQ, HD), F32),
        vm((MICRO, SEQ, HD), F32),
        vm((T * MICRO * LOC, D), F32),
        vm((NX, 2, MICRO * LOC, D), BF16),
        *[vm((2, MICRO * LOC, D), BF16) for _ in range(4)],
        vm((MICRO * LOC, D), BF16),
        vm((MICRO * LOC, D), BF16),
        vm((NX, MICRO * LOC, D), BF16),
        vm((MICRO * LOC, D), F32),
        vm((MICRO, LOC, D), BF16),
        dma((9,)),
        dma((PH,)),
        dma((PH, 4)),
        dma((PH,)),
        dma((PH, 4, 4, 2)),
        dma((PH,)),
        dma((PH, 4, 2)),
        dma((PH,)),
        dma((PH, 4)),
        dma((PH,)),
        dma((PH,)),
        dma((3,)),
        dma((9,)),
        dma((NB, 2)),
        dma((NB, 7)),
    ]
    return pl.pallas_call(
        body,
        name="layer",
        out_shape=(
            jax.ShapeDtypeStruct((MICRO, SEQ, QC), BF16),
            jax.ShapeDtypeStruct((MICRO, LOC, D), BF16),
        ),
        in_specs=[
            anyspec, anyspec, anyspec, pl.BlockSpec(memory_space=pltpu.SMEM), anyspec,
        ],
        out_specs=(anyspec, anyspec),
        scratch_shapes=scratch,
        compiler_params=pltpu.CompilerParams(
            collective_id=0, has_side_effects=True, vmem_limit_bytes=56 << 20
        ),
        cost_estimate=pl.CostEstimate(flops=7_500_000_000, bytes_accessed=5_000_000, transcendentals=1_000_000),
    )(x_in, w_in, kv2, lens, d_in)


def solution(mesh):
    return jax.shard_map(
        run,
        mesh=mesh,
        in_specs=(
            P(None, ("dp", "tensor"), None),
            P("dp", "tensor"),
            P(None, None, "tensor"),
            P("dp", None, None),
            P(None, "dp", "tensor"),
        ),
        out_specs=(P(None, "dp", "tensor"), P(None, ("dp", "tensor"), None)),
        check_vma=False,
    )
```

time: 113 us -> 99.6 us (0.88)
  Pallas kernels: 107 us -> 95.2 us
  local copies, waits for them, and re-layouts: 4.84 us -> 3.59 us
    pallas_call x1, Pallas kernels: 107 us -> 95.2 us  [run(): pl.pallas_call(body, name='layer', out_shape=(jax.ShapeDtypeStruct((MICRO...]
    another operation x1 -> x0, local copies, waits for them, and re-layouts: 1.25 us -> none
where the time goes in v2:
time: 99.6 us; the launch traced here: 99.4 us
  Pallas kernels  95.2 us (96%)
  local copies, waits for them, and re-layouts  3.59 us (4%)
    pallas_call x1, Pallas kernels, run(): pl.pallas_call(body, name='layer', out_shape=(jax.ShapeDtypeStruct((MICRO...  95.2 us
    unnamed x2, local copies, waits for them, and re-layouts  3.59 us

profile of v2, /device:TPU:1, one launch (start us, length us, event | category | flops | bytes accessed | tf_op | source)
XLA Modules:
  0.0 99.4 jit_solution(13317771396984933663)
XLA Ops:
  0.6 95.2 %layer.1 = (bf16[2,128,1024]{2,1,0:T(8,128)(2,1)}, bf16[2,16,5120]{2,1,0:T(8,128)(2,1)}) custom-call(bf16[2,16,5120]{2,1,0:T(8,128)(2,1)} %x_hbm.1, bf16[80,1024]{1,0:T(8,128)(2,1)} %w_hbm.1, bf16[10240,128]{1,0:T(8,128)(2,1)} %bitcast.1, s32[1,2,4]{2,1,0:T(2,128)} %len_ref.1, bf16[2,128,1024]{2,1,0:T(8,128)(2,1)} %dctx_hbm.1), custom_call_target="tpu_custom_call" | custom-call | flops 7500000256 | bytes 5000000 | tf_op jit(solution)/shard_map/layer/pallas_call | solution.py:532
  95.8 1.9 %copy.9 = bf16[2,128,1024]{2,1,0:T(8,128)(2,1)} copy(bf16[2,128,1024]{2,1,0:T(8,128)(2,1)} %get-tuple-element.4) | data formatting | bytes 1048576
  97.7 1.7 %copy.10 = bf16[2,16,5120]{2,1,0:T(8,128)(2,1)} copy(bf16[2,16,5120]{2,1,0:T(8,128)(2,1)} %get-tuple-element.5) | data formatting | bytes 655360
